TPU v7x, 256 devices: a whole 4x4x8 slice. The times are simulated.
256 devices in a mesh: group: 32 (over z, y_hi, core), seq: 8 (over x, y_lo).
Axes of the slice: x: 4, y: 4 (y_hi: 2, y_lo: 2; y = y_hi * 2 + y_lo), z: 8, core: 2. Of those that a mesh axis runs over, the one named last changes fastest.
Arguments:
- spatial_qkv: bfloat16 [32, 8, 512, 4608], P('group', 'seq'), may hold values from -6 to 6
- temporal_qkv: bfloat16 [32, 8, 512, 4608], P('group', 'seq'), may hold values from -6 to 6
- caption_kv: bfloat16 [32, 1024, 3072], P(None, 'group'), may hold values from -6 to 6
- frame_count: int32 [32], P('group'), may hold values from 1 to 8, as said below
- caption_len: int32 [32], P('group'), may hold values from 1 to 1024, as said below
Outputs:
- attn_mix: bfloat16 [32, 8, 512, 1536], P('group', 'seq')
Inputs may be any that keep to these rules, and one draw needn't show every extreme that they name: `frame_count`: each video has 1 to 8 frames with data, the first ones; some video has all 8. `caption_len`: each caption has 1 to 1024 tokens with data, the first ones; some caption has all 1024.
All inputs are finite; a program needn't handle non-finite values.
Results may differ from a plain program's by a relative error of at most 0.012.
Values may be sent and summed in bfloat16 or wider, within the bound.
A program may use at most 192 MiB of HBM per device.

v0:
```python
import jax
import jax.numpy as jnp
from jax import lax
from jax.sharding import PartitionSpec as P

HD = 128


NEG_FILL = -1e30


def soft_weights(scores):
    row_top = jnp.max(scores, axis=-1, keepdims=True)
    lifted = jnp.exp(scores - row_top)
    return (lifted / jnp.sum(lifted, axis=-1, keepdims=True)).astype(jnp.bfloat16)


def attend(queries, keys_in, values, key_valid):
    scores = jnp.einsum(
        "mhe,khe->hmk", queries, keys_in, preferred_element_type=jnp.float32
    ) * HD ** (-0.5)
    scores = jnp.where(key_valid[None, None, :], scores, NEG_FILL)
    weights = soft_weights(scores)
    return jnp.einsum("hmk,khe->mhe", weights, values, preferred_element_type=jnp.float32)


def temporal_attend(queries, keys_in, values, frame_total):
    frame_slots = keys_in.shape[0]
    scores = jnp.einsum(
        "fphe,gphe->phfg", queries, keys_in, preferred_element_type=jnp.float32
    ) * HD ** (-0.5)
    frame_valid = jnp.arange(frame_slots) < frame_total
    scores = jnp.where(frame_valid[None, None, None, :], scores, NEG_FILL)
    weights = soft_weights(scores)
    return jnp.einsum(
        "phfg,gphe->fphe", weights, values, preferred_element_type=jnp.float32
    ).astype(jnp.bfloat16)


def split_three(block, feat_width, head_count):
    lead = block.shape[:-1]
    queries = block[..., :feat_width].reshape(lead + (head_count, HD))
    keys_in = block[..., feat_width : 2 * feat_width].reshape(lead + (head_count, HD))
    values = block[..., 2 * feat_width :].reshape(lead + (head_count, HD))
    return (queries, keys_in, values)


def body(spatial_qkv, temporal_qkv, caption_kv, frame_count, caption_len):
    frames_dev = spatial_qkv.shape[1]
    tokens = spatial_qkv.shape[2]
    feat_width = spatial_qkv.shape[3] // 3
    head_count = feat_width // HD
    seq_rank = lax.axis_index("seq")
    frame_total = frame_count[0]
    caption_total = caption_len[0]
    caption_all = lax.all_to_all(caption_kv, "group", split_axis=0, concat_axis=1, tiled=True)
    cap_tokens = caption_all.shape[1]
    cap_keys = caption_all[0, :, :feat_width].reshape(cap_tokens, head_count, HD)
    cap_values = caption_all[0, :, feat_width:].reshape(cap_tokens, head_count, HD)
    cap_valid = jnp.arange(cap_tokens) < caption_total
    all_tokens = jnp.ones((tokens,), dtype=bool)

    def frame_mix(frame_rows):
        queries, keys_in, values = split_three(frame_rows, feat_width, head_count)
        return attend(queries, keys_in, values, all_tokens) + attend(
            queries, cap_keys, cap_values, cap_valid
        )

    frame_ids = seq_rank * frames_dev + jnp.arange(frames_dev)
    local_mix = lax.map(frame_mix, spatial_qkv[0])
    regrouped = lax.all_to_all(temporal_qkv, "seq", split_axis=2, concat_axis=1, tiled=True)
    frame_slots = regrouped.shape[1]
    spots = regrouped.shape[2]
    queries, keys_in, values = split_three(regrouped[0], feat_width, head_count)
    attended = temporal_attend(queries, keys_in, values, frame_total)
    returned = lax.all_to_all(
        attended.reshape(1, frame_slots, spots, feat_width),
        "seq",
        split_axis=1,
        concat_axis=2,
        tiled=True,
    )
    temporal_out = returned[0].reshape(frames_dev, tokens, head_count, HD)
    widened = lax.optimization_barrier(temporal_out).astype(jnp.float32)
    frame_valid = (frame_ids < frame_total).astype(jnp.float32)
    mixed = (local_mix + widened) * frame_valid[:, None, None, None]
    return mixed.reshape(1, frames_dev, tokens, feat_width).astype(jnp.bfloat16)


def solution(mesh):
    placed = (
        P("group", "seq", None, None),
        P("group", "seq", None, None),
        P(None, "group", None),
        P("group"),
        P("group"),
    )
    return jax.shard_map(
        body, mesh=mesh, in_specs=placed, out_specs=P("group", "seq", None, None), check_vma=False
    )
```

profile of v0, /device:TPU:1, one launch (start us, length us, event | category | flops | bytes accessed | tf_op | source)
XLA Modules:
  0.0 382.6 jit_solution(17019082944229055988)
XLA Ops:
  0.0 9.6 %copy.107 = bf16[1,1,512,4608]{3,1,0,2:T(2,128)(2,1)} copy(bf16[1,1,512,4608]{3,2,1,0:T(8,128)(2,1)} %param.6) | data formatting | bytes 9437184 | tf_op args[1]
  10.1 32.0 %reduce = bf16[512,4608]{1,0:T(8,128)(2,1)} reduce(bf16[512,1,1,4608]{3,2,1,0:T(2,128)(2,1)} %bitcast.45, bf16[]{:T(256)} %broadcast.44), dimensions={1,2}, to_apply=%bitcast.42.reduce_sub_computation | reduce | bytes 9437186
  42.0 8.2 %reshape.76 = bf16[8,2,147456]{2,1,0:T(2,128)(2,1)} reshape(bf16[512,4608]{1,0:T(8,128)(2,1)} %reduce) | data formatting | bytes 9437184
  50.2 5.9 %all-to-all-start.1 = ((bf16[8,2,147456]{2,1,0:T(2,128)(2,1)}), bf16[8,2,147456]{2,1,0:T(2,128)(2,1)}, u32[]{:S(2)}, u32[]{:S(2)}) async-start(bf16[8,2,147456]{2,1,0:T(2,128)(2,1)} %reshape.76), calls=%async_computation.1 | async-start | bytes 9437184 | tf_op jit(solution)/shard_map/all_to_all | solution.py:71
  56.7 64.8 %all-to-all-done.1 = bf16[8,2,147456]{2,1,0:T(2,128)(2,1)} async-done(((bf16[8,2,147456]{2,1,0:T(2,128)(2,1)}), bf16[8,2,147456]{2,1,0:T(2,128)(2,1)}, u32[]{:S(2)}, u32[]{:S(2)}) %all-to-all-start.1) | async-done | bytes 4718624 | tf_op jit(solution)/shard_map/all_to_all | solution.py:71
  121.6 9.3 %reshape.77 = bf16[512,1,1,4608]{3,2,1,0:T(2,128)(2,1)} reshape(bf16[8,2,147456]{2,1,0:T(2,128)(2,1)} %all-to-all-done.1) | data formatting | bytes 9437184
  130.9 4.7 %copy.97 = bf16[1,1,512,4608]{3,2,0,1:T(8,128)(2,1)S(1)} copy(bf16[1,1,512,4608]{3,1,0,2:T(2,128)(2,1)} %bitcast.46) | data formatting | bytes 9437184
  141.4 4.1 %fusion.16 = f32[64,12,8,8]{2,3,1,0:T(8,128)S(1)} fusion(bf16[8,64,12,128]{3,2,1,0:T(8,128)(2,1)} %reshape.72, bf16[8,64,12,128]{3,2,1,0:T(8,128)(2,1)} %reshape.71), kind=kOutput, calls=%fused_computation.22 | convolution fusion | flops 12582912 | bytes 3342336 | tf_op jit(solution)/shard_map/fphe,gphe->phfg/dot_general | solution.py:29
  149.4 2.9 reshape.73
  152.3 2.6 fusion.19
  157.2 22.7 %all_to_all.30 = bf16[1,8,64,1536]{3,2,0,1:T(8,128)(2,1)} all-to-all(bf16[1,8,64,1536]{3,2,0,1:T(8,128)(2,1)} %bitcast.49), channel_id=1, replica_groups=mesh['group'=32,'seq'=8] {'seq'}, dimensions={1} | all-to-all | bytes 3145728 | tf_op jit(solution)/shard_map/all_to_all | solution.py:76
  179.9 15.0 %all-to-all-start = ((bf16[32,32,3072]{2,1,0:T(8,128)(2,1)}), bf16[32,32,3072]{2,1,0:T(8,128)(2,1)}, u32[]{:S(2)}, u32[]{:S(2)}) async-start(bf16[32,32,3072]{2,1,0:T(8,128)(2,1)} %param.7), calls=%async_computation | async-start | bytes 12582912 | tf_op jit(solution)/shard_map/all_to_all | solution.py:56
  195.5 6.7 %copy.74 = bf16[1,1,512,4608]{2,3,1,0:T(8,128)(2,1)} copy(bf16[1,1,512,4608]{3,2,1,0:T(8,128)(2,1)} %param.5) | data formatting | bytes 9437184 | tf_op args[0]
  202.3 3.9 %fusion.38 = (bf16[512,1536]{0,1:T(8,128)(2,1)S(1)}, bf16[512,1536]{0,1:T(8,128)(2,1)}, bf16[512,1536]{0,1:T(8,128)(2,1)S(1)}) fusion(bf16[512,4608]{0,1:T(8,128)(2,1)} %bitcast.48), kind=kLoop, calls=%fused_computation.44 | loop fusion | bytes 9437184 | tf_op jit(solution)/shard_map/while/body/eval_jaxpr/slice | solution.py:43
  207.4 7.1 %fusion.42 = (f32[12,512]{1,0:T(8,128)S(1)}, f32[12,512,512]{1,2,0:T(8,128)}) fusion(bf16[512,12,128]{0,2,1:T(8,128)(2,1)S(1)} %bitcast.53, bf16[512,12,128]{0,2,1:T(8,128)(2,1)S(1)} %bitcast.55), kind=kOutput, calls=%fused_computation.48 | convolution fusion | flops 814744064 | bytes 15753216 | tf_op jit(solution)/shard_map/while/body/eval_jaxpr/sub | solution.py:14
  214.4 2.9 reshape_squeeze.11
  217.3 2.6 copy.90
  219.9 116.6 %all-to-all-done = bf16[32,32,3072]{2,1,0:T(8,128)(2,1)} async-done(((bf16[32,32,3072]{2,1,0:T(8,128)(2,1)}), bf16[32,32,3072]{2,1,0:T(8,128)(2,1)}, u32[]{:S(2)}, u32[]{:S(2)}) %all-to-all-start) | async-done | bytes 6291488 | tf_op jit(solution)/shard_map/all_to_all | solution.py:56
  336.5 4.9 %fusion.37 = (bf16[1,1024,1536]{2,1,0:T(8,128)(2,1)S(1)}, bf16[1,1024,1536]{2,1,0:T(8,128)(2,1)}) fusion(bf16[1,1024,3072]{2,1,0:T(8,128)(2,1)} %bitcast.5), kind=kLoop, calls=%fused_computation.43 | loop fusion | bytes 12582912 | tf_op jit(solution)/shard_map/slice | solution.py:58
  341.5 4.7 %copy.81 = bf16[1,1024,1536]{1,2,0:T(8,128)(2,1)} copy(bf16[1,1024,1536]{2,1,0:T(8,128)(2,1)} %get-tuple-element.16) | data formatting | bytes 6291456 | tf_op jit(solution)/shard_map/slice | solution.py:59
  346.1 3.0 copy.78
  349.1 14.6 %fusion.41 = (f32[12,512]{1,0:T(8,128)S(1)}, f32[12,512,1024]{2,1,0:T(8,128)}) fusion(pred[1024]{0:T(1024)(128)(4,1)S(1)} %iota_compare_fusion, bf16[512,12,128]{0,2,1:T(8,128)(2,1)} %bitcast.54, bf16[1024,12,128]{0,2,1:T(8,128)(2,1)} %bitcast.51), kind=kOutput, calls=%fused_computation.47 | convolution fusion | flops 1635779584 | bytes 29910016 | tf_op jit(solution)/shard_map/while/body/eval_jaxpr/sub | solution.py:14
  363.7 10.9 %fusion.7 = f32[12,512,128]{1,2,0:T(8,128)S(1)} fusion(bf16[1024,12,128]{0,2,1:T(8,128)(2,1)S(1)} %bitcast.50, f32[12,512,1024]{2,1,0:T(8,128)} %get-tuple-element.34, f32[12,512]{1,0:T(8,128)S(1)} %get-tuple-element.33), kind=kOutput, calls=%fused_computation.12 | convolution fusion | flops 1623195648 | bytes 31481856 | tf_op jit(solution)/shard_map/while/body/eval_jaxpr/hmk,khe->mhe/dot_general | solution.py:24
  374.6 6.4 %fusion.14 = bf16[1,512,12,128]{1,3,2,0:T(8,128)(2,1)S(1)} fusion(bf16[1,512,12,128]{1,3,2,0:T(8,128)(2,1)S(1)} %copy-done.2, f32[12,512,128]{1,2,0:T(8,128)S(1)} %fusion.7, bf16[512,12,128]{0,2,1:T(8,128)(2,1)S(1)} %bitcast.52, f32[12,512,512]{1,2,0:T(8,128)} %get-tuple-element.36, f32[12,512]{1,0:T(8,128)S(1)} %get-tuple-element.35, f32[]{:T(128)} %bitcast.14), kind=kOutput, calls=%fused_computation.19 | convolution fusion | flops 815529984 | bytes 20471812 | tf_op jit(solution)/shard_map/while/body/eval_jaxpr/hmk,khe->mhe/dot_general | solution.py:24
  (21 shorter events, 15.3 us)
Async XLA Ops:
  50.2 71.4 %all-to-all-start.1 = ((bf16[8,2,147456]{2,1,0:T(2,128)(2,1)}), bf16[8,2,147456]{2,1,0:T(2,128)(2,1)}, u32[]{:S(2)}, u32[]{:S(2)}) async-start(bf16[8,2,147456]{2,1,0:T(2,128)(2,1)} %reshape.76), calls=%async_computation.1 | async-start | bytes 9437184 | tf_op jit(solution)/shard_map/all_to_all | solution.py:71
  179.9 156.7 %all-to-all-start = ((bf16[32,32,3072]{2,1,0:T(8,128)(2,1)}), bf16[32,32,3072]{2,1,0:T(8,128)(2,1)}, u32[]{:S(2)}, u32[]{:S(2)}) async-start(bf16[32,32,3072]{2,1,0:T(8,128)(2,1)} %param.7), calls=%async_computation | async-start | bytes 12582912 | tf_op jit(solution)/shard_map/all_to_all | solution.py:56
  206.2 1.2 copy-start.3
  349.1 14.6 %copy-start = (bf16[1,1024,1536]{1,2,0:T(8,128)(2,1)S(1)}, bf16[1,1024,1536]{1,2,0:T(8,128)(2,1)}, u32[]{:S(2)}) copy-start(bf16[1,1024,1536]{1,2,0:T(8,128)(2,1)} %copy.81) | copy-start | bytes 9437188
  363.7 10.9 %copy-start.1 = (bf16[512,1536]{0,1:T(8,128)(2,1)S(1)}, bf16[512,1536]{0,1:T(8,128)(2,1)}, u32[]{:S(2)}) copy-start(bf16[512,1536]{0,1:T(8,128)(2,1)} %get-tuple-element.24) | copy-start | bytes 4718596
  363.7 10.9 %copy-start.2 = (bf16[1,512,12,128]{1,3,2,0:T(8,128)(2,1)S(1)}, bf16[1,512,12,128]{1,3,2,0:T(8,128)(2,1)}, u32[]{:S(2)}) copy-start(bf16[1,512,12,128]{1,3,2,0:T(8,128)(2,1)} %copy.90) | copy-start | bytes 4718596
where the time goes:
time: 384 us; the launch traced here: 383 us
  waiting for transfers between devices  181 us (47%)
  local copies, waits for them, and re-layouts  78.2 us (20%)
  matrix products  45.6 us (12%)
  other arithmetic  32.4 us (8%)
  blocking collectives  22.7 us (6%)
  starting transfers between devices  20.9 us (5%)
    all_to_all x1, waiting for transfers between devices, body(): lax.all_to_all(caption_kv, 'group', split_axis=0, concat_axis=1, tiled=True)  117 us
    all_to_all x1, waiting for transfers between devices, body(): lax.all_to_all(temporal_qkv, 'seq', split_axis=2, concat_axis=1, tiled=True)  64.8 us
    unnamed x14, local copies, waits for them, and re-layouts  40.1 us
    unnamed x1, other arithmetic  32 us
    all_to_all x1, blocking collectives, body(): lax.all_to_all(attended.reshape(1, frame_slots, spots, feat_width), 'seq'...  22.7 us
    sub x2, matrix products, soft_weights(): lifted = jnp.exp(scores - row_top)  21.6 us
    dot_general x2, matrix products, attend(): jnp.einsum('hmk,khe->mhe', weights, values, preferred_element_type=jnp.fl...  17.3 us
    all_to_all x1, starting transfers between devices, body(): lax.all_to_all(caption_kv, 'group', split_axis=0, concat_axis=1, tiled=True)  15 us
  transfers between devices with their start and end apart: 2, of which 2 were waited for; matrix products, arithmetic and copies ran while one was open for 6% of the time, Pallas kernels for 0%

commit v1 on v0

v1 whole, which is shorter than its diff:
```python
import functools

import jax
import jax.numpy as jnp
from jax import lax
from jax.experimental import pallas as pl
from jax.experimental.pallas import tpu as pltpu
from jax.sharding import PartitionSpec as P

HD = 128
PAIR = 2 * HD
NEG_FILL = -1e30
LOG2E = 1.4426950408889634
MESH = pl.DeviceIdType.MESH
SETS = 3
ROWS_T = 16
BLOCK = 256


def nt(a, b):
    return lax.dot_general(a, b, (((1,), (1,)), ((), ())), preferred_element_type=jnp.float32)


def soft_apply(scores, values):
    top = jnp.max(scores, axis=-1, keepdims=True)
    lifted = jnp.exp2((scores - top) * (HD ** -0.5 * LOG2E)).astype(jnp.bfloat16)
    wide = jnp.concatenate([values, jnp.ones_like(values)], axis=1)
    mixed = jnp.dot(lifted, wide, preferred_element_type=jnp.float32)
    return mixed[:, :HD] / mixed[:, HD:]


def kernel(
    dims,
    fc_ref, cl_ref, sp_ref, tq_ref, cap_ref,
    out_ref,
    spv, trecv, tsend, tret, capkv, qpart, xsend, xret, acc,
    local_sem, t_s, t_r, r_s, r_r, c_s, c_r, q_s, q_r, x_s, x_r,
):
    groups, seqs, tokens, feat = dims
    heads = feat // HD
    g = lax.axis_index("group")
    s = lax.axis_index("seq")
    x, yl = s // 2, s % 2
    yh = (g // 2) % 2
    par = x % 2
    spots = tokens // seqs
    chunks = spots // ROWS_T
    cap_rows = cap_ref.shape[1]
    cap_tokens = groups * cap_rows
    partners = ((x + 1 - 2 * par) * 2 + yl, (3 - x) * 2 + yl, x * 2 + 1 - yl)
    mine = (4 * par, 4 * par + 2, 8 + 2 * yl)
    theirs = (4 - 4 * par, 6 - 4 * par, 10 - 2 * yl)

    def col(head):
        return pl.multiple_of(head * HD, HD)

    def seq_peer(i):
        return lax.rem(s + i, seqs)

    def group_peer(i):
        half = (i + 2) // 2
        offset = half + (i % 2) * (groups - 2 * half)
        peer = lax.rem(g + offset, groups)
        flip = ((peer // 2) % 2 + yh) % 2
        return peer, (yl + flip) % 2

    barrier = pltpu.get_barrier_semaphore()

    @pl.loop(1, seqs)
    def _(i):
        pl.semaphore_signal(barrier, inc=1, device_id=(g, seq_peer(i)), device_id_type=MESH)

    @pl.loop(0, groups - 1)
    def _(i):
        peer, peer_yl = group_peer(i)
        pl.semaphore_signal(barrier, inc=1, device_id=(peer, x * 2 + peer_yl), device_id_type=MESH)

    load_spatial = pltpu.make_async_copy(sp_ref.at[0, 0], spv, local_sem.at[0])
    load_spatial.start()
    pl.semaphore_wait(barrier, seqs - 1 + groups - 1)

    for i in range(SETS):
        pltpu.make_async_remote_copy(
            src_ref=sp_ref.at[0, 0, :, pl.ds(col(theirs[i]), PAIR)],
            dst_ref=qpart.at[i],
            send_sem=q_s,
            recv_sem=q_r.at[i],
            device_id=(g, partners[i]),
            device_id_type=MESH,
        ).start()

    def send_temporal(j):
        @pl.loop(1, seqs)
        def _(i):
            peer = seq_peer(i)
            pltpu.make_async_remote_copy(
                src_ref=tq_ref.at[0, 0, pl.ds(pl.multiple_of(peer * spots + j * ROWS_T, ROWS_T), ROWS_T)],
                dst_ref=trecv.at[j, s],
                send_sem=t_s,
                recv_sem=t_r.at[j],
                device_id=(g, peer),
                device_id_type=MESH,
            ).start()

    def send_captions(i):
        @pl.loop(0, groups - 1)
        def _(n):
            peer, peer_yl = group_peer(n)
            first = mine[i] if i < 2 else 8 + 2 * peer_yl
            for part in range(2):
                pltpu.make_async_remote_copy(
                    src_ref=cap_ref.at[peer, :, pl.ds(col(first + part * heads), PAIR)],
                    dst_ref=capkv.at[i, part, pl.ds(pl.multiple_of(g * cap_rows, cap_rows), cap_rows)],
                    send_sem=c_s,
                    recv_sem=c_r.at[i],
                    device_id=(peer, x * 2 + peer_yl),
                    device_id_type=MESH,
                ).start()

    for j in range(chunks):
        send_temporal(j)
        if j < SETS:
            send_captions(j)

    own = [
        pltpu.make_async_copy(
            tq_ref.at[0, 0, pl.ds(pl.multiple_of(s * spots + j * ROWS_T, ROWS_T), ROWS_T)],
            trecv.at[j, s],
            local_sem.at[1 + j],
        )
        for j in range(chunks)
    ]
    for copy in own:
        copy.start()
    own_cap = []
    for i in range(SETS):
        for part in range(2):
            copy = pltpu.make_async_copy(
                cap_ref.at[g, :, pl.ds(col(mine[i] + part * heads), PAIR)],
                capkv.at[i, part, pl.ds(pl.multiple_of(g * cap_rows, cap_rows), cap_rows)],
                local_sem.at[1 + chunks + 2 * i + part],
            )
            copy.start()
            own_cap.append(copy)

    def landed(ref, sem):
        pltpu.make_async_copy(ref, ref, sem).wait()

    frame_total = fc_ref[0]
    caption_total = cl_ref[0]

    load_spatial.wait()

    def spatial(first, count):
        @pl.loop(first, first + count)
        def _(h):
            keys_in = spv[:, pl.ds(col(heads + h), HD)]
            values = spv[:, pl.ds(col(2 * heads + h), HD)]
            for b in range(tokens // BLOCK):
                rows = pl.ds(b * BLOCK, BLOCK)
                acc[rows, pl.ds(col(h), HD)] = soft_apply(nt(spv[rows, pl.ds(col(h), HD)], keys_in), values)

    def temporal(j):
        own[j].wait()
        landed(trecv.at[j, pl.ds(0, seqs - 1)], t_r.at[j])
        size = seqs * ROWS_T
        row = lax.broadcasted_iota(jnp.int32, (size, size), 0)
        column = lax.broadcasted_iota(jnp.int32, (size, size), 1)
        keep = ((row % ROWS_T) == (column % ROWS_T)) & (column // ROWS_T < frame_total)

        @pl.loop(0, heads)
        def _(h):
            q, k, v = (
                trecv[j, :, :, pl.ds(col(part * heads + h), HD)].reshape(size, HD) for part in range(3)
            )
            mixed = soft_apply(jnp.where(keep, nt(q, k), NEG_FILL), v)
            tsend[j, :, :, pl.ds(col(h), HD)] = mixed.astype(jnp.bfloat16).reshape(seqs, ROWS_T, HD)

        home = pl.ds(pl.multiple_of(s * spots + j * ROWS_T, ROWS_T), ROWS_T)

        @pl.loop(1, seqs)
        def _(i):
            peer = seq_peer(i)
            pltpu.make_async_remote_copy(
                src_ref=tsend.at[j, peer],
                dst_ref=tret.at[home],
                send_sem=r_s,
                recv_sem=r_r,
                device_id=(g, peer),
                device_id_type=MESH,
            ).start()

        tret[home] = tsend[j, s]

    def cross(i):
        landed(qpart.at[i], q_r.at[i])
        own_cap[2 * i].wait()
        own_cap[2 * i + 1].wait()
        landed(capkv.at[i, :, pl.ds(0, cap_tokens - cap_rows)], c_r.at[i])
        token = lax.broadcasted_iota(jnp.int32, (1, cap_tokens), 1)
        bias = jnp.where(token < caption_total, 0.0, NEG_FILL)
        for k in range(2):
            lanes = pl.ds(k * HD, HD)

            @pl.loop(0, tokens // BLOCK)
            def _(b):
                rows = pl.ds(pl.multiple_of(b * BLOCK, BLOCK), BLOCK)
                scores = nt(qpart[i, rows, lanes], capkv[i, 0, :, lanes]) + bias
                xsend[i, rows, lanes] = soft_apply(scores, capkv[i, 1, :, lanes]).astype(jnp.bfloat16)

        pltpu.make_async_remote_copy(
            src_ref=xsend.at[i],
            dst_ref=xret.at[i],
            send_sem=x_s,
            recv_sem=x_r.at[i],
            device_id=(g, partners[i]),
            device_id_type=MESH,
        ).start()
        for k in range(2):
            lanes = pl.ds(k * HD, HD)
            head = pl.ds(col(mine[i] + k), HD)

            @pl.loop(0, tokens // BLOCK)
            def _(b):
                rows = pl.ds(pl.multiple_of(b * BLOCK, BLOCK), BLOCK)
                scores = nt(spv[rows, head], capkv[i, 0, :, lanes]) + bias
                acc[rows, head] += soft_apply(scores, capkv[i, 1, :, lanes])

    spatial(0, heads)
    temporal(0)
    cross(0)
    temporal(1)
    temporal(2)
    cross(1)
    temporal(3)
    cross(2)

    landed(tret.at[pl.ds(0, tokens - spots)], r_r)
    keep_frame = (s + jnp.zeros((1, 1), jnp.int32)) < frame_total

    def write(lanes, extra):
        total = acc[:, lanes] + tret[:, lanes].astype(jnp.float32)
        if extra is not None:
            total += extra
        out_ref[0, 0, :, lanes] = jnp.where(keep_frame, total, 0.0).astype(jnp.bfloat16)

    for i in range(SETS):
        write(pl.ds(col(mine[i]), PAIR), None)
    for i in range(SETS):
        landed(xret.at[i], x_r.at[i])
        write(pl.ds(col(theirs[i]), PAIR), xret[i].astype(jnp.float32))

    landed(trecv.at[:, pl.ds(0, seqs - 1)], t_s)
    landed(tsend.at[:, pl.ds(0, seqs - 1)], r_s)
    landed(capkv.at[:, :, pl.ds(0, cap_tokens - cap_rows)], c_s)
    landed(qpart, q_s)
    landed(xsend, x_s)


def body(dims, spatial_qkv, temporal_qkv, caption_kv, frame_count, caption_len):
    groups, seqs, tokens, feat = dims
    spots = tokens // seqs
    chunks = spots // ROWS_T
    cap_tokens = groups * caption_kv.shape[1]
    bf16 = jnp.bfloat16
    dma = pltpu.SemaphoreType.DMA
    return pl.pallas_call(
        functools.partial(kernel, dims),
        out_shape=jax.ShapeDtypeStruct((1, 1, tokens, feat), bf16),
        in_specs=[pl.BlockSpec(memory_space=pltpu.SMEM)] * 2 + [pl.BlockSpec(memory_space=pl.ANY)] * 3,
        out_specs=pl.BlockSpec(memory_space=pltpu.VMEM),
        scratch_shapes=[
            pltpu.VMEM((tokens, 3 * feat), bf16),
            pltpu.VMEM((chunks, seqs, ROWS_T, 3 * feat), bf16),
            pltpu.VMEM((chunks, seqs, ROWS_T, feat), bf16),
            pltpu.VMEM((tokens, feat), bf16),
            pltpu.VMEM((SETS, 2, cap_tokens, PAIR), bf16),
            pltpu.VMEM((SETS, tokens, PAIR), bf16),
            pltpu.VMEM((SETS, tokens, PAIR), bf16),
            pltpu.VMEM((SETS, tokens, PAIR), bf16),
            pltpu.VMEM((tokens, feat), jnp.float32),
            dma((1 + chunks + 2 * SETS,)),
            dma, dma((chunks,)),
            dma, dma,
            dma, dma((SETS,)),
            dma, dma((SETS,)),
            dma, dma((SETS,)),
        ],
        compiler_params=pltpu.CompilerParams(
            collective_id=0, has_side_effects=True, vmem_limit_bytes=56 << 20
        ),
    )(frame_count, caption_len, spatial_qkv, temporal_qkv, caption_kv)


def solution(mesh):
    groups, seqs = mesh.shape["group"], mesh.shape["seq"]
    placed = (
        P("group", "seq", None, None),
        P("group", "seq", None, None),
        P(None, "group", None),
        P("group"),
        P("group"),
    )

    def whole(spatial_qkv, *rest):
        dims = (groups, seqs, spatial_qkv.shape[2], spatial_qkv.shape[3] // 3)
        return jax.shard_map(
            functools.partial(body, dims),
            mesh=mesh,
            in_specs=placed,
            out_specs=P("group", "seq", None, None),
            check_vma=False,
        )(spatial_qkv, *rest)

    return whole
```

time: 384 us -> 110 us (0.29)
  waiting for transfers between devices: 181 us -> 0 us
  Pallas kernels: 0 us -> 106 us
  local copies, waits for them, and re-layouts: 78.2 us -> 2.65 us
  matrix products: 45.6 us -> 0 us
  other arithmetic: 32.4 us -> 0 us
  blocking collectives: 22.7 us -> 0 us
  starting transfers between devices: 20.9 us -> 0 us
    all_to_all x2 -> x0, waiting for transfers between devices: 181 us -> none  [the longest x1 117 us: body(): lax.all_to_all(caption_kv, 'group', split_axis=0, concat_axis=1, tiled=True)]
    pallas_call x0 -> x1, Pallas kernels: none -> 106 us  [body(): pl.pallas_call(functools.partial(kernel, dims), out_shape=jax.ShapeDtypeS...]
    unnamed x14 -> x1, local copies, waits for them, and re-layouts: 40.1 us -> 2.65 us
    unnamed x1 -> x0, other arithmetic: 32 us -> none
    dot_general x4 -> x0, matrix products: 24 us -> none  [the longest x2 17.3 us: attend(): jnp.einsum('hmk,khe->mhe', weights, values, preferred_element_type=jnp.fl...]
    all_to_all x1 -> x0, blocking collectives: 22.7 us -> none  [body(): lax.all_to_all(attended.reshape(1, frame_slots, spots, feat_width), 'seq'...]
    sub x2 -> x0, matrix products: 21.6 us -> none  [soft_weights(): lifted = jnp.exp(scores - row_top)]
    all_to_all x2 -> x0, starting transfers between devices: 20.9 us -> none  [the longest x1 15 us: body(): lax.all_to_all(caption_kv, 'group', split_axis=0, concat_axis=1, tiled=True)]
  transfers between devices with their start and end apart: 2 -> 0, of which waited for: 2 -> 0; matrix products, arithmetic and copies ran while one was open for 6% -> 0% of each run, Pallas kernels for 0% -> 0%
where the time goes in v1:
time: 110 us
  Pallas kernels  106 us (96%)
  local copies, waits for them, and re-layouts  2.65 us (2%)
  between operations  1.3 us (1%)
    pallas_call x1, Pallas kernels, body(): pl.pallas_call(functools.partial(kernel, dims), out_shape=jax.ShapeDtypeS...  106 us
    unnamed x1, local copies, waits for them, and re-layouts  2.65 us

profile of v1, /device:TPU:1, one launch (start us, length us, event | category | flops | bytes accessed | tf_op | source)
XLA Modules:
  0.0 109.9 jit_solution(6635527174222849753)
XLA Ops:
  1.3 105.9 %shard_map.55 = bf16[1,1,512,1536]{3,2,1,0:T(8,128)(2,1)} custom-call(s32[1]{0:T(128)S(6)} %copy.7.fc_ref, s32[1]{0:T(128)S(6)} %copy.8.cl_ref, bf16[1,1,512,4608]{3,2,1,0:T(8,128)(2,1)} %sp_ref.1, bf16[1,1,512,4608]{3,2,1,0:T(8,128)(2,1)} %tq_ref.1, bf16[32,32,3072]{2,1,0:T(8,128)(2,1)} %cap_ref.1), custom_call_target="tpu_custom_call" | custom-call | tf_op jit(solution)/shard_map/pallas_call | solution.py:267
  107.2 2.7 %copy.9 = bf16[1,1,512,1536]{3,2,1,0:T(8,128)(2,1)} copy(bf16[1,1,512,1536]{3,2,1,0:T(8,128)(2,1)} %shard_map.55) | data formatting | bytes 3145728

commit v2 on v1

v2 whole, which is shorter than its diff:
```python
import functools

import jax
import jax.numpy as jnp
from jax import lax
from jax.experimental import pallas as pl
from jax.experimental.pallas import tpu as pltpu
from jax.sharding import PartitionSpec as P

HD = 128
PAIR = 2 * HD
NEG_FILL = -1e30
LOG2E = 1.4426950408889634
MESH = pl.DeviceIdType.MESH
SETS = 3
ROWS_T = 16
UNROLL = 4


def nt(a, b):
    return lax.dot_general(a, b, (((1,), (1,)), ((), ())), preferred_element_type=jnp.float32)


def lift(scores, top):
    return jnp.exp2((scores - top) * (HD ** -0.5 * LOG2E))


def attend(queries, keys_in, values, bias=None):
    half = keys_in.shape[0] // 2
    top = None
    for part in range(2):
        span = slice(part * half, (part + 1) * half)
        scores = nt(queries, keys_in[span])
        if bias is not None:
            scores = scores + bias[:, span]
        peak = jnp.max(scores, axis=-1, keepdims=True)
        new_top = peak if top is None else jnp.maximum(top, peak)
        lifted = lift(scores, new_top)
        summed = jnp.sum(lifted, axis=-1, keepdims=True)
        mixed = jnp.dot(lifted.astype(jnp.bfloat16), values[span], preferred_element_type=jnp.float32)
        if top is not None:
            fade = lift(top, new_top)
            summed += total * fade
            mixed += out * fade
        top, total, out = new_top, summed, mixed
    return out / total


def attend_kept(queries, keys_in, values, keep):
    turned = keys_in.astype(jnp.float32).T.astype(jnp.bfloat16)
    scores = jnp.where(keep, jnp.dot(queries, turned, preferred_element_type=jnp.float32), NEG_FILL)
    lifted = lift(scores, jnp.max(scores, axis=-1, keepdims=True))
    mixed = jnp.dot(lifted.astype(jnp.bfloat16), values, preferred_element_type=jnp.float32)
    return mixed / jnp.sum(lifted, axis=-1, keepdims=True)


def kernel(
    dims,
    fc_ref, cl_ref, sp_ref, tq_ref, cap_ref,
    out_ref,
    spv, trecv, yrelay, tsend, rrelay, tret, capkv, hrelay, qpart, xsend, xret, acc,
    local_sem, y_s, y_r, t_s, f_s, t_r, a_s, b_s, b_r, g_s, r_r, h_s, h_r, c_s, d_s, c_r, q_s, q_r, x_s, x_r,
):
    groups, seqs, tokens, feat = dims
    heads = feat // HD
    xs, zs = seqs // 2, groups // 4
    g = lax.axis_index("group")
    s = lax.axis_index("seq")
    x, yl = s // 2, s % 2
    z, yh, core = g // 4, (g // 2) % 2, g % 2
    par = x % 2
    spots = tokens // seqs
    chunks = spots // ROWS_T
    cap_rows = cap_ref.shape[3]
    cap_tokens = groups * cap_rows
    y_seq = x * 2 + 1 - yl
    hi_dev = ((z * 2 + 1 - yh) * 2 + core, x * 2 + 1 - yl)
    partners = (y_seq, (x + 1 - 2 * par) * 2 + yl, (3 - x) * 2 + yl)
    mine = (8 + 2 * yl, 4 * par, 4 * par + 2)
    theirs = (10 - 2 * yl, 4 - 4 * par, 6 - 4 * par)
    hi_mine = (10 - 2 * yl, 4 * par, 4 * par + 2)

    def col(head):
        return pl.multiple_of(head * HD, HD)

    def x_peer(dx):
        return lax.rem(x + dx, xs)

    def z_peer(n):
        i = n // 2
        half = (i + 2) // 2
        offset = half + (i % 2) * (zs - 2 * half)
        last = n // (2 * zs - 2)
        return lax.rem(z + offset * (1 - last), zs), lax.rem(core + n + last, 2)

    def send(src, dst, send_sem, recv_sem, device):
        pltpu.make_async_remote_copy(
            src_ref=src, dst_ref=dst, send_sem=send_sem, recv_sem=recv_sem, device_id=device, device_id_type=MESH
        ).start()

    def landed(ref, sem):
        pltpu.make_async_copy(ref, ref, sem).wait()

    barrier = pltpu.get_barrier_semaphore()

    def greet(device):
        pl.semaphore_signal(barrier, inc=1, device_id=device, device_id_type=MESH)

    @pl.loop(1, xs)
    def _(dx):
        greet((g, x_peer(dx) * 2 + yl))

    greet((g, y_seq))
    greet(hi_dev)

    @pl.loop(0, 2 * zs - 1)
    def _(n):
        pz, pc = z_peer(n)
        greet(((pz * 2 + yh) * 2 + pc, s))

    load_spatial = pltpu.make_async_copy(sp_ref.at[0, 0], spv, local_sem.at[0])
    load_spatial.start()
    pl.semaphore_wait(barrier, xs - 1 + 2 + 2 * zs - 1)

    def spot_rows(owner, j):
        return pl.ds(pl.multiple_of(owner * spots + j * ROWS_T, ROWS_T), ROWS_T)

    def send_queries(i):
        send(sp_ref.at[0, 0, :, pl.ds(col(theirs[i]), PAIR)], qpart.at[i], q_s, q_r.at[i], (g, partners[i]))

    def send_y(j):
        @pl.loop(1, xs)
        def _(dx):
            owner = x_peer(dx) * 2 + 1 - yl
            send(tq_ref.at[0, 0, spot_rows(owner, j)], yrelay.at[j, dx - 1], y_s, y_r.at[j, dx - 1], (g, y_seq))

        send(tq_ref.at[0, 0, spot_rows(y_seq, j)], trecv.at[j, s], y_s, t_r.at[j], (g, y_seq))

    def send_x(j):
        @pl.loop(1, xs)
        def _(dx):
            owner = x_peer(dx) * 2 + yl
            send(tq_ref.at[0, 0, spot_rows(owner, j)], trecv.at[j, s], t_s, t_r.at[j], (g, owner))

    def pass_x(j):
        @pl.loop(1, xs)
        def _(dx):
            landed(yrelay.at[j, dx - 1], y_r.at[j, dx - 1])
            send(yrelay.at[j, dx - 1], trecv.at[j, y_seq], f_s, t_r.at[j], (g, x_peer(dx) * 2 + yl))

    def cap_slot(group):
        return pl.ds(pl.multiple_of(group * cap_rows, cap_rows), cap_rows)

    def send_hi(i):
        for part in range(2):
            send(
                cap_ref.at[:, 1 - yh, :, :, pl.ds(col(hi_mine[i] + part * heads), PAIR)],
                hrelay.at[i, :, :, part],
                h_s,
                h_r.at[i],
                hi_dev,
            )

    def send_z(i):
        @pl.loop(0, 2 * zs - 1)
        def _(n):
            pz, pc = z_peer(n)
            for part in range(2):
                send(
                    cap_ref.at[pz, yh, pc, :, pl.ds(col(mine[i] + part * heads), PAIR)],
                    capkv.at[i, part, cap_slot(g)],
                    c_s,
                    c_r.at[i],
                    ((pz * 2 + yh) * 2 + pc, s),
                )

    def own_z(i, part):
        return pltpu.make_async_copy(
            cap_ref.at[z, yh, core, :, pl.ds(col(mine[i] + part * heads), PAIR)],
            capkv.at[i, part, cap_slot(g)],
            local_sem.at[1 + chunks + 2 * i + part],
        )

    def own_pass(i):
        return pltpu.make_async_copy(
            hrelay.at[i, z, core], capkv.at[i, :, cap_slot(hi_dev[0])], local_sem.at[1 + chunks + 2 * SETS + i]
        )

    def pass_z(i):
        landed(hrelay.at[i], h_r.at[i])

        @pl.loop(0, 2 * zs - 1)
        def _(n):
            pz, pc = z_peer(n)
            send(
                hrelay.at[i, pz, pc],
                capkv.at[i, :, cap_slot(hi_dev[0])],
                d_s,
                c_r.at[i],
                ((pz * 2 + yh) * 2 + pc, s),
            )

        own_pass(i).start()

    def own_t(j):
        return pltpu.make_async_copy(tq_ref.at[0, 0, spot_rows(s, j)], trecv.at[j, s], local_sem.at[1 + j])

    frame_total = fc_ref[0]
    caption_total = cl_ref[0]

    def spatial(first, count):
        @pl.loop(first, first + count)
        def _(h):
            q, k, v = (spv[:, pl.ds(col(part * heads + h), HD)] for part in range(3))
            acc[:, pl.ds(col(h), HD)] = attend(q, k, v)

    def temporal(j):
        own_t(j).wait()
        landed(trecv.at[j, pl.ds(0, seqs - 1)], t_r.at[j])
        size = seqs * ROWS_T
        row = lax.broadcasted_iota(jnp.int32, (size, size), 0)
        column = lax.broadcasted_iota(jnp.int32, (size, size), 1)
        keep = ((row % ROWS_T) == (column % ROWS_T)) & (column // ROWS_T < frame_total)

        @pl.loop(0, heads // UNROLL)
        def _(n):
            for u in range(UNROLL):
                h = n * UNROLL + u
                q, k, v = (
                    trecv[j, :, :, pl.ds(col(part * heads + h), HD)].reshape(size, HD) for part in range(3)
                )
                mixed = attend_kept(q, k, v, keep)
                tsend[j, :, :, pl.ds(col(h), HD)] = mixed.astype(jnp.bfloat16).reshape(seqs, ROWS_T, HD)

        home = spot_rows(s, j)
        send(tsend.at[j, y_seq], tret.at[home], b_s, r_r, (g, y_seq))

        @pl.loop(1, xs)
        def _(dx):
            send(tsend.at[j, x_peer(dx) * 2 + 1 - yl], rrelay.at[j, dx - 1], b_s, b_r.at[j], (g, y_seq))

        @pl.loop(1, xs)
        def _(dx):
            peer = x_peer(dx) * 2 + yl
            send(tsend.at[j, peer], tret.at[home], a_s, r_r, (g, peer))

        tret[home] = tsend[j, s]

    def pass_back(j):
        landed(rrelay.at[j], b_r.at[j])

        @pl.loop(1, xs)
        def _(dx):
            send(rrelay.at[j, dx - 1], tret.at[spot_rows(y_seq, j)], g_s, r_r, (g, x_peer(dx) * 2 + yl))

    token = lax.broadcasted_iota(jnp.int32, (1, cap_tokens), 1)
    bias = jnp.where(token < caption_total, 0.0, NEG_FILL)

    def cross_theirs(i):
        landed(qpart.at[i], q_r.at[i])
        own_z(i, 0).wait()
        own_z(i, 1).wait()
        own_pass(i).wait()
        landed(capkv.at[i, :, pl.ds(0, cap_tokens - 2 * cap_rows)], c_r.at[i])
        @pl.loop(0, 2)
        def _(k):
            lanes = pl.ds(col(k), HD)
            mixed = attend(qpart[i, :, lanes], capkv[i, 0, :, lanes], capkv[i, 1, :, lanes], bias)
            xsend[i, :, lanes] = mixed.astype(jnp.bfloat16)

    def send_cross(i):
        send(xsend.at[i], xret.at[i], x_s, x_r.at[i], (g, partners[i]))

    def cross_mine(i):
        @pl.loop(0, 2)
        def _(k):
            lanes = pl.ds(col(k), HD)
            head = pl.ds(col(mine[i] + k), HD)
            acc[:, head] += attend(spv[:, head], capkv[i, 0, :, lanes], capkv[i, 1, :, lanes], bias)

    send_y(0)
    send_x(0)
    send_hi(0)
    send_z(0)
    send_queries(0)
    send_y(1)
    send_x(1)
    send_hi(1)
    send_queries(1)
    send_queries(2)
    send_z(1)
    send_y(2)
    send_y(3)
    send_hi(2)
    for j in range(chunks):
        own_t(j).start()
    for i in range(SETS):
        own_z(i, 0).start()
        own_z(i, 1).start()
    load_spatial.wait()
    spatial(0, 6)
    pass_x(0)
    send_x(2)
    pass_z(0)
    send_z(2)
    spatial(6, 6)
    pass_z(1)
    pass_x(1)
    send_x(3)
    temporal(0)
    pass_z(2)
    cross_theirs(0)
    cross_mine(0)
    pass_x(2)
    temporal(1)
    pass_x(3)
    temporal(2)
    cross_theirs(1)
    send_cross(1)
    pass_back(0)
    temporal(3)
    send_cross(0)
    cross_mine(1)
    pass_back(1)
    pass_back(2)
    cross_theirs(2)
    send_cross(2)
    pass_back(3)
    cross_mine(2)

    landed(tret.at[pl.ds(0, tokens - spots)], r_r)
    keep_frame = (s + jnp.zeros((1, 1), jnp.int32)) < frame_total

    def write(lanes, extra):
        total = acc[:, lanes] + tret[:, lanes].astype(jnp.float32)
        if extra is not None:
            total += extra
        out_ref[0, 0, :, lanes] = jnp.where(keep_frame, total, 0.0).astype(jnp.bfloat16)

    for i in range(SETS):
        write(pl.ds(col(mine[i]), PAIR), None)
    for i in range(SETS):
        landed(xret.at[i], x_r.at[i])
        write(pl.ds(col(theirs[i]), PAIR), xret[i].astype(jnp.float32))

    landed(trecv.at[:, pl.ds(0, xs)], y_s)
    landed(trecv.at[:, pl.ds(0, xs - 1)], t_s)
    landed(yrelay, f_s)
    landed(tsend.at[:, pl.ds(0, xs)], b_s)
    landed(tsend.at[:, pl.ds(0, xs - 1)], a_s)
    landed(rrelay, g_s)
    landed(capkv.at[:, :, pl.ds(0, (2 * zs - 1) * cap_rows)], c_s)
    landed(capkv.at[:, :, pl.ds(0, (2 * zs - 1) * cap_rows)], d_s)
    landed(hrelay, h_s)
    landed(qpart, q_s)
    landed(xsend, x_s)


def body(dims, spatial_qkv, temporal_qkv, caption_kv, frame_count, caption_len):
    groups, seqs, tokens, feat = dims
    spots = tokens // seqs
    chunks = spots // ROWS_T
    cap_rows = caption_kv.shape[1]
    cap_tokens = groups * cap_rows
    caption_kv = caption_kv.reshape(groups // 4, 2, 2, cap_rows, 2 * feat)
    bf16 = jnp.bfloat16
    dma = pltpu.SemaphoreType.DMA
    return pl.pallas_call(
        functools.partial(kernel, dims),
        out_shape=jax.ShapeDtypeStruct((1, 1, tokens, feat), bf16),
        in_specs=[pl.BlockSpec(memory_space=pltpu.SMEM)] * 2 + [pl.BlockSpec(memory_space=pl.ANY)] * 3,
        out_specs=pl.BlockSpec(memory_space=pltpu.VMEM),
        scratch_shapes=[
            pltpu.VMEM((tokens, 3 * feat), bf16),
            pltpu.VMEM((chunks, seqs, ROWS_T, 3 * feat), bf16),
            pltpu.VMEM((chunks, seqs // 2 - 1, ROWS_T, 3 * feat), bf16),
            pltpu.VMEM((chunks, seqs, ROWS_T, feat), bf16),
            pltpu.VMEM((chunks, seqs // 2 - 1, ROWS_T, feat), bf16),
            pltpu.VMEM((tokens, feat), bf16),
            pltpu.VMEM((SETS, 2, cap_tokens, PAIR), bf16),
            pltpu.VMEM((SETS, groups // 4, 2, 2, cap_rows, PAIR), bf16),
            pltpu.VMEM((SETS, tokens, PAIR), bf16),
            pltpu.VMEM((SETS, tokens, PAIR), bf16),
            pltpu.VMEM((SETS, tokens, PAIR), bf16),
            pltpu.VMEM((tokens, feat), jnp.float32),
            dma((1 + chunks + 3 * SETS,)),
            dma, dma((chunks, seqs // 2 - 1)),
            dma, dma, dma((chunks,)),
            dma, dma, dma((chunks,)), dma, dma,
            dma, dma((SETS,)),
            dma, dma, dma((SETS,)),
            dma, dma((SETS,)),
            dma, dma((SETS,)),
        ],
        compiler_params=pltpu.CompilerParams(
            collective_id=0, has_side_effects=True, vmem_limit_bytes=56 << 20
        ),
    )(frame_count, caption_len, spatial_qkv, temporal_qkv, caption_kv)


def solution(mesh):
    groups, seqs = mesh.shape["group"], mesh.shape["seq"]
    placed = (
        P("group", "seq", None, None),
        P("group", "seq", None, None),
        P(None, "group", None),
        P("group"),
        P("group"),
    )

    def whole(spatial_qkv, *rest):
        dims = (groups, seqs, spatial_qkv.shape[2], spatial_qkv.shape[3] // 3)
        return jax.shard_map(
            functools.partial(body, dims),
            mesh=mesh,
            in_specs=placed,
            out_specs=P("group", "seq", None, None),
            check_vma=False,
        )(spatial_qkv, *rest)

    return whole
```

time: 110 us -> 102 us (0.927)
  Pallas kernels: 106 us -> 97.9 us
    pallas_call x1, Pallas kernels: 106 us -> 97.9 us  [body(): pl.pallas_call(functools.partial(kernel, dims), out_shape=jax.ShapeDtypeS...]
where the time goes in v2:
time: 102 us
  Pallas kernels  97.9 us (96%)
  local copies, waits for them, and re-layouts  2.65 us (3%)
  between operations  1.3 us (1%)
    pallas_call x1, Pallas kernels, body(): pl.pallas_call(functools.partial(kernel, dims), out_shape=jax.ShapeDtypeS...  97.9 us
    unnamed x1, local copies, waits for them, and re-layouts  2.65 us

profile of v2, /device:TPU:1, one launch (start us, length us, event | category | flops | bytes accessed | tf_op | source)
XLA Modules:
  0.0 101.9 jit_solution(17288415409887210083)
XLA Ops:
  1.3 97.9 %shard_map.55 = bf16[1,1,512,1536]{3,2,1,0:T(8,128)(2,1)} custom-call(s32[1]{0:T(128)S(6)} %copy.7.fc_ref, s32[1]{0:T(128)S(6)} %copy.8.cl_ref, bf16[1,1,512,4608]{3,2,1,0:T(8,128)(2,1)} %sp_ref.1, bf16[1,1,512,4608]{3,2,1,0:T(8,128)(2,1)} %tq_ref.1, bf16[8,2,2,32,3072]{4,3,2,1,0:T(8,128)(2,1)} %bitcast.1), custom_call_target="tpu_custom_call" | custom-call | tf_op jit(solution)/shard_map/pallas_call | solution.py:368
  99.2 2.7 %copy.9 = bf16[1,1,512,1536]{3,2,1,0:T(8,128)(2,1)} copy(bf16[1,1,512,1536]{3,2,1,0:T(8,128)(2,1)} %shard_map.55) | data formatting | bytes 3145728

commit v3 on v2

--- a/solution.py
+++ b/solution.py
@@ -13,6 +13,7 @@
 LOG2E = 1.4426950408889634
 MESH = pl.DeviceIdType.MESH
 SETS = 3
+PARCELS = ((0, 0, 2), (1, 0, 2), (2, 0, 1), (2, 1, 1))
 ROWS_T = 16
 UNROLL = 4
 
@@ -59,7 +60,7 @@
     fc_ref, cl_ref, sp_ref, tq_ref, cap_ref,
     out_ref,
     spv, trecv, yrelay, tsend, rrelay, tret, capkv, hrelay, qpart, xsend, xret, acc,
-    local_sem, y_s, y_r, t_s, f_s, t_r, a_s, b_s, b_r, g_s, r_r, h_s, h_r, c_s, d_s, c_r, q_s, q_r, x_s, x_r,
+    near_sem, far_sem, local_sem, y_s, y_r, t_s, f_s, t_r, a_s, b_s, b_r, g_s, r_r, h_s, h_r, c_s, d_s, c_r, q_s, q_r, x_s, x_r,
 ):
     groups, seqs, tokens, feat = dims
     heads = feat // HD
@@ -102,25 +103,48 @@
         pltpu.make_async_copy(ref, ref, sem).wait()
 
     barrier = pltpu.get_barrier_semaphore()
+    first_core = g - core
+    other_core = (first_core + 1 - core, s)
 
     def greet(device):
         pl.semaphore_signal(barrier, inc=1, device_id=device, device_id_type=MESH)
 
     @pl.loop(1, xs)
     def _(dx):
-        greet((g, x_peer(dx) * 2 + yl))
-
-    greet((g, y_seq))
-    greet(hi_dev)
-
-    @pl.loop(0, 2 * zs - 1)
-    def _(n):
-        pz, pc = z_peer(n)
-        greet(((pz * 2 + yh) * 2 + pc, s))
+        greet((first_core, x_peer(dx) * 2 + yl))
+
+    greet((first_core, y_seq))
+    greet((hi_dev[0] - core, hi_dev[1]))
+
+    @pl.loop(1, zs)
+    def _(dz):
+        greet(((lax.rem(z + dz, zs) * 2 + yh) * 2 + 1, s))
+
+    @pl.when(core == 1)
+    def _():
+        greet(other_core)
 
     load_spatial = pltpu.make_async_copy(sp_ref.at[0, 0], spv, local_sem.at[0])
     load_spatial.start()
-    pl.semaphore_wait(barrier, xs - 1 + 2 + 2 * zs - 1)
+
+    @pl.when(core == 0)
+    def _():
+        pl.semaphore_wait(barrier, 2 * (xs + 1) + 1)
+        pl.semaphore_signal(near_sem, inc=1, device_id=other_core, device_id_type=MESH)
+
+    @pl.when(core == 1)
+    def _():
+        pl.semaphore_wait(near_sem, 1)
+
+    def wait_far():
+        @pl.when(core == 1)
+        def _():
+            pl.semaphore_wait(barrier, 2 * (zs - 1))
+            pl.semaphore_signal(far_sem, inc=1, device_id=other_core, device_id_type=MESH)
+
+        @pl.when(core == 0)
+        def _():
+            pl.semaphore_wait(far_sem, 1)
 
     def spot_rows(owner, j):
         return pl.ds(pl.multiple_of(owner * spots + j * ROWS_T, ROWS_T), ROWS_T)
@@ -151,26 +175,32 @@
     def cap_slot(group):
         return pl.ds(pl.multiple_of(group * cap_rows, cap_rows), cap_rows)
 
-    def send_hi(i):
+    def lanes_of(p):
+        return pl.ds(PARCELS[p][1] * HD, PARCELS[p][2] * HD)
+
+    def send_hi(p):
+        i, first, count = PARCELS[p]
         for part in range(2):
             send(
-                cap_ref.at[:, 1 - yh, :, :, pl.ds(col(hi_mine[i] + part * heads), PAIR)],
-                hrelay.at[i, :, :, part],
+                cap_ref.at[:, 1 - yh, :, :, pl.ds(col(hi_mine[i] + first + part * heads), count * HD)],
+                hrelay.at[i, :, :, part, :, lanes_of(p)],
                 h_s,
-                h_r.at[i],
+                h_r.at[p],
                 hi_dev,
             )
 
-    def send_z(i):
+    def send_z(p):
+        i, first, count = PARCELS[p]
+
         @pl.loop(0, 2 * zs - 1)
         def _(n):
             pz, pc = z_peer(n)
             for part in range(2):
                 send(
-                    cap_ref.at[pz, yh, pc, :, pl.ds(col(mine[i] + part * heads), PAIR)],
-                    capkv.at[i, part, cap_slot(g)],
+                    cap_ref.at[pz, yh, pc, :, pl.ds(col(mine[i] + first + part * heads), count * HD)],
+                    capkv.at[i, part, cap_slot(g), lanes_of(p)],
                     c_s,
-                    c_r.at[i],
+                    c_r.at[p],
                     ((pz * 2 + yh) * 2 + pc, s),
                 )
 
@@ -181,26 +211,30 @@
             local_sem.at[1 + chunks + 2 * i + part],
         )
 
-    def own_pass(i):
+    def own_pass(p):
+        i = PARCELS[p][0]
         return pltpu.make_async_copy(
-            hrelay.at[i, z, core], capkv.at[i, :, cap_slot(hi_dev[0])], local_sem.at[1 + chunks + 2 * SETS + i]
+            hrelay.at[i, z, core, :, :, lanes_of(p)],
+            capkv.at[i, :, cap_slot(hi_dev[0]), lanes_of(p)],
+            local_sem.at[1 + chunks + 2 * SETS + p],
         )
 
-    def pass_z(i):
-        landed(hrelay.at[i], h_r.at[i])
+    def pass_z(p):
+        i = PARCELS[p][0]
+        landed(hrelay.at[i, :, :, :, :, lanes_of(p)], h_r.at[p])
 
         @pl.loop(0, 2 * zs - 1)
         def _(n):
             pz, pc = z_peer(n)
             send(
-                hrelay.at[i, pz, pc],
-                capkv.at[i, :, cap_slot(hi_dev[0])],
+                hrelay.at[i, pz, pc, :, :, lanes_of(p)],
+                capkv.at[i, :, cap_slot(hi_dev[0]), lanes_of(p)],
                 d_s,
-                c_r.at[i],
+                c_r.at[p],
                 ((pz * 2 + yh) * 2 + pc, s),
             )
 
-        own_pass(i).start()
+        own_pass(p).start()
 
     def own_t(j):
         return pltpu.make_async_copy(tq_ref.at[0, 0, spot_rows(s, j)], trecv.at[j, s], local_sem.at[1 + j])
@@ -233,11 +267,12 @@
                 tsend[j, :, :, pl.ds(col(h), HD)] = mixed.astype(jnp.bfloat16).reshape(seqs, ROWS_T, HD)
 
         home = spot_rows(s, j)
+
+        @pl.loop(1, xs)
+        def _(dx):
+            send(tsend.at[j, x_peer(dx) * 2 + 1 - yl], rrelay.at[j, dx - 1], b_s, b_r.at[j, dx - 1], (g, y_seq))
+
         send(tsend.at[j, y_seq], tret.at[home], b_s, r_r, (g, y_seq))
-
-        @pl.loop(1, xs)
-        def _(dx):
-            send(tsend.at[j, x_peer(dx) * 2 + 1 - yl], rrelay.at[j, dx - 1], b_s, b_r.at[j], (g, y_seq))
 
         @pl.loop(1, xs)
         def _(dx):
@@ -247,32 +282,37 @@
         tret[home] = tsend[j, s]
 
     def pass_back(j):
-        landed(rrelay.at[j], b_r.at[j])
-
-        @pl.loop(1, xs)
-        def _(dx):
+        @pl.loop(1, xs)
+        def _(dx):
+            landed(rrelay.at[j, dx - 1], b_r.at[j, dx - 1])
             send(rrelay.at[j, dx - 1], tret.at[spot_rows(y_seq, j)], g_s, r_r, (g, x_peer(dx) * 2 + yl))
 
     token = lax.broadcasted_iota(jnp.int32, (1, cap_tokens), 1)
     bias = jnp.where(token < caption_total, 0.0, NEG_FILL)
 
-    def cross_theirs(i):
-        landed(qpart.at[i], q_r.at[i])
-        own_z(i, 0).wait()
-        own_z(i, 1).wait()
-        own_pass(i).wait()
-        landed(capkv.at[i, :, pl.ds(0, cap_tokens - 2 * cap_rows)], c_r.at[i])
-        @pl.loop(0, 2)
+    def cross_theirs(p):
+        i, first, count = PARCELS[p]
+        if first == 0:
+            landed(qpart.at[i], q_r.at[i])
+            own_z(i, 0).wait()
+            own_z(i, 1).wait()
+        own_pass(p).wait()
+        landed(capkv.at[i, :, pl.ds(0, cap_tokens - 2 * cap_rows), lanes_of(p)], c_r.at[p])
+
+        @pl.loop(first, first + count)
         def _(k):
             lanes = pl.ds(col(k), HD)
             mixed = attend(qpart[i, :, lanes], capkv[i, 0, :, lanes], capkv[i, 1, :, lanes], bias)
             xsend[i, :, lanes] = mixed.astype(jnp.bfloat16)
 
-    def send_cross(i):
-        send(xsend.at[i], xret.at[i], x_s, x_r.at[i], (g, partners[i]))
-
-    def cross_mine(i):
-        @pl.loop(0, 2)
+    def send_cross(p):
+        i = PARCELS[p][0]
+        send(xsend.at[i, :, lanes_of(p)], xret.at[i, :, lanes_of(p)], x_s, x_r.at[p], (g, partners[i]))
+
+    def cross_mine(p):
+        i, first, count = PARCELS[p]
+
+        @pl.loop(first, first + count)
         def _(k):
             lanes = pl.ds(col(k), HD)
             head = pl.ds(col(mine[i] + k), HD)
@@ -281,38 +321,43 @@
     send_y(0)
     send_x(0)
     send_hi(0)
-    send_z(0)
     send_queries(0)
     send_y(1)
     send_x(1)
     send_hi(1)
     send_queries(1)
     send_queries(2)
-    send_z(1)
     send_y(2)
     send_y(3)
     send_hi(2)
+    send_hi(3)
     for j in range(chunks):
         own_t(j).start()
     for i in range(SETS):
         own_z(i, 0).start()
         own_z(i, 1).start()
+    wait_far()
+    send_z(0)
+    send_z(1)
     load_spatial.wait()
-    spatial(0, 6)
+    spatial(0, 4)
     pass_x(0)
     send_x(2)
     pass_z(0)
     send_z(2)
-    spatial(6, 6)
+    spatial(4, 4)
     pass_z(1)
     pass_x(1)
     send_x(3)
+    send_z(3)
+    spatial(8, 4)
     temporal(0)
     pass_z(2)
+    pass_x(2)
     cross_theirs(0)
     cross_mine(0)
-    pass_x(2)
     temporal(1)
+    pass_z(3)
     pass_x(3)
     temporal(2)
     cross_theirs(1)
@@ -325,8 +370,11 @@
     pass_back(2)
     cross_theirs(2)
     send_cross(2)
+    cross_mine(2)
     pass_back(3)
-    cross_mine(2)
+    cross_theirs(3)
+    send_cross(3)
+    cross_mine(3)
 
     landed(tret.at[pl.ds(0, tokens - spots)], r_r)
     keep_frame = (s + jnp.zeros((1, 1), jnp.int32)) < frame_total
@@ -339,9 +387,9 @@
 
     for i in range(SETS):
         write(pl.ds(col(mine[i]), PAIR), None)
-    for i in range(SETS):
-        landed(xret.at[i], x_r.at[i])
-        write(pl.ds(col(theirs[i]), PAIR), xret[i].astype(jnp.float32))
+    for p, (i, first, count) in enumerate(PARCELS):
+        landed(xret.at[i, :, lanes_of(p)], x_r.at[p])
+        write(pl.ds(col(theirs[i] + first), count * HD), xret[i, :, lanes_of(p)].astype(jnp.float32))
 
     landed(trecv.at[:, pl.ds(0, xs)], y_s)
     landed(trecv.at[:, pl.ds(0, xs - 1)], t_s)
@@ -367,7 +415,7 @@
     dma = pltpu.SemaphoreType.DMA
     return pl.pallas_call(
         functools.partial(kernel, dims),
-        out_shape=jax.ShapeDtypeStruct((1, 1, tokens, feat), bf16),
+        out_shape=pltpu.VMEM((1, 1, tokens, feat), bf16),
         in_specs=[pl.BlockSpec(memory_space=pltpu.SMEM)] * 2 + [pl.BlockSpec(memory_space=pl.ANY)] * 3,
         out_specs=pl.BlockSpec(memory_space=pltpu.VMEM),
         scratch_shapes=[
@@ -383,14 +431,16 @@
             pltpu.VMEM((SETS, tokens, PAIR), bf16),
             pltpu.VMEM((SETS, tokens, PAIR), bf16),
             pltpu.VMEM((tokens, feat), jnp.float32),
-            dma((1 + chunks + 3 * SETS,)),
+            pltpu.SemaphoreType.REGULAR,
+            pltpu.SemaphoreType.REGULAR,
+            dma((1 + chunks + 2 * SETS + len(PARCELS),)),
             dma, dma((chunks, seqs // 2 - 1)),
             dma, dma, dma((chunks,)),
-            dma, dma, dma((chunks,)), dma, dma,
+            dma, dma, dma((chunks, seqs // 2 - 1)), dma, dma,
+            dma, dma((len(PARCELS),)),
+            dma, dma, dma((len(PARCELS),)),
             dma, dma((SETS,)),
-            dma, dma, dma((SETS,)),
-            dma, dma((SETS,)),
-            dma, dma((SETS,)),
+            dma, dma((len(PARCELS),)),
         ],
         compiler_params=pltpu.CompilerParams(
             collective_id=0, has_side_effects=True, vmem_limit_bytes=56 << 20

time: 102 us -> 94.4 us (0.925)
  Pallas kernels: 97.9 us -> 91.9 us
  local copies, waits for them, and re-layouts: 2.65 us -> 1.15 us
    pallas_call x1, Pallas kernels: 97.9 us -> 91.9 us  [body(): pl.pallas_call(functools.partial(kernel, dims), out_shape=pltpu.VMEM((1,...]
    unnamed x1, local copies, waits for them, and re-layouts: 2.65 us -> 1.15 us
where the time goes in v3:
time: 94.4 us
  Pallas kernels  91.9 us (97%)
  between operations  1.31 us (1%)
  local copies, waits for them, and re-layouts  1.15 us (1%)
    pallas_call x1, Pallas kernels, body(): pl.pallas_call(functools.partial(kernel, dims), out_shape=pltpu.VMEM((1,...  91.9 us

profile of v3, /device:TPU:1, one launch (start us, length us, event | category | flops | bytes accessed | tf_op | source)
XLA Modules:
  0.0 94.4 jit_solution(15332007115142532048)
XLA Ops:
  1.3 91.9 %shard_map.55 = bf16[1,1,512,1536]{3,2,1,0:T(8,128)(2,1)S(1)} custom-call(s32[1]{0:T(128)S(6)} %copy.8.fc_ref, s32[1]{0:T(128)S(6)} %copy.9.cl_ref, bf16[1,1,512,4608]{3,2,1,0:T(8,128)(2,1)} %sp_ref.1, bf16[1,1,512,4608]{3,2,1,0:T(8,128)(2,1)} %tq_ref.1, bf16[8,2,2,32,3072]{4,3,2,1,0:T(8,128)(2,1)} %bitcast.1), custom_call_target="tpu_custom_call" | custom-call | tf_op jit(solution)/shard_map/pallas_call | solution.py:416
  93.2 1.1 %copy.7 = bf16[1,1,512,1536]{3,2,1,0:T(8,128)(2,1)} copy(bf16[1,1,512,1536]{3,2,1,0:T(8,128)(2,1)S(1)} %shard_map.55) | data formatting | bytes 3145728

commit v4 on v3

--- a/solution.py
+++ b/solution.py
@@ -76,10 +76,10 @@
     cap_tokens = groups * cap_rows
     y_seq = x * 2 + 1 - yl
     hi_dev = ((z * 2 + 1 - yh) * 2 + core, x * 2 + 1 - yl)
-    partners = (y_seq, (x + 1 - 2 * par) * 2 + yl, (3 - x) * 2 + yl)
-    mine = (8 + 2 * yl, 4 * par, 4 * par + 2)
-    theirs = (10 - 2 * yl, 4 - 4 * par, 6 - 4 * par)
-    hi_mine = (10 - 2 * yl, 4 * par, 4 * par + 2)
+    partners = ((x + 1 - 2 * par) * 2 + yl, (3 - x) * 2 + yl, y_seq)
+    mine = (4 * par, 4 * par + 2, 8 + 2 * yl)
+    theirs = (4 - 4 * par, 6 - 4 * par, 10 - 2 * yl)
+    hi_mine = (4 * par, 4 * par + 2, 10 - 2 * yl)
 
     def col(head):
         return pl.multiple_of(head * HD, HD)
@@ -321,14 +321,14 @@
     send_y(0)
     send_x(0)
     send_hi(0)
-    send_queries(0)
     send_y(1)
     send_x(1)
     send_hi(1)
+    send_queries(0)
     send_queries(1)
-    send_queries(2)
     send_y(2)
     send_y(3)
+    send_queries(2)
     send_hi(2)
     send_hi(3)
     for j in range(chunks):
@@ -350,30 +350,31 @@
     pass_x(1)
     send_x(3)
     send_z(3)
-    spatial(8, 4)
     temporal(0)
     pass_z(2)
+    spatial(8, 2)
     pass_x(2)
+    temporal(1)
     cross_theirs(0)
-    cross_mine(0)
-    temporal(1)
     pass_z(3)
+    spatial(10, 2)
     pass_x(3)
+    send_cross(0)
     temporal(2)
     cross_theirs(1)
     send_cross(1)
     pass_back(0)
     temporal(3)
-    send_cross(0)
+    cross_mine(0)
+    pass_back(1)
     cross_mine(1)
-    pass_back(1)
     pass_back(2)
     cross_theirs(2)
     send_cross(2)
-    cross_mine(2)
     pass_back(3)
     cross_theirs(3)
     send_cross(3)
+    cross_mine(2)
     cross_mine(3)
 
     landed(tret.at[pl.ds(0, tokens - spots)], r_r)

time: 94.4 us -> 91.5 us (0.969)
  Pallas kernels: 91.9 us -> 89 us
    pallas_call x1, Pallas kernels: 91.9 us -> 89 us  [body(): pl.pallas_call(functools.partial(kernel, dims), out_shape=pltpu.VMEM((1,...]
where the time goes in v4:
time: 91.5 us
  Pallas kernels  89 us (97%)
  between operations  1.31 us (1%)
  local copies, waits for them, and re-layouts  1.15 us (1%)
    pallas_call x1, Pallas kernels, body(): pl.pallas_call(functools.partial(kernel, dims), out_shape=pltpu.VMEM((1,...  89 us

profile of v4, /device:TPU:1, one launch (start us, length us, event | category | flops | bytes accessed | tf_op | source)
XLA Modules:
  0.0 91.5 jit_solution(9411224389737641364)
XLA Ops:
  1.3 89.0 %shard_map.55 = bf16[1,1,512,1536]{3,2,1,0:T(8,128)(2,1)S(1)} custom-call(s32[1]{0:T(128)S(6)} %copy.8.fc_ref, s32[1]{0:T(128)S(6)} %copy.9.cl_ref, bf16[1,1,512,4608]{3,2,1,0:T(8,128)(2,1)} %sp_ref.1, bf16[1,1,512,4608]{3,2,1,0:T(8,128)(2,1)} %tq_ref.1, bf16[8,2,2,32,3072]{4,3,2,1,0:T(8,128)(2,1)} %bitcast.1), custom_call_target="tpu_custom_call" | custom-call | tf_op jit(solution)/shard_map/pallas_call | solution.py:417
  90.3 1.1 %copy.7 = bf16[1,1,512,1536]{3,2,1,0:T(8,128)(2,1)} copy(bf16[1,1,512,1536]{3,2,1,0:T(8,128)(2,1)S(1)} %shard_map.55) | data formatting | bytes 3145728

commit v5 on v4

--- a/solution.py
+++ b/solution.py
@@ -57,10 +57,10 @@
 
 def kernel(
     dims,
-    fc_ref, cl_ref, sp_ref, tq_ref, cap_ref,
+    fc_hbm, cl_hbm, sp_ref, tq_ref, cap_ref,
     out_ref,
     spv, trecv, yrelay, tsend, rrelay, tret, capkv, hrelay, qpart, xsend, xret, acc,
-    near_sem, far_sem, local_sem, y_s, y_r, t_s, f_s, t_r, a_s, b_s, b_r, g_s, r_r, h_s, h_r, c_s, d_s, c_r, q_s, q_r, x_s, x_r,
+    fc_ref, cl_ref, near_sem, far_sem, scalar_sem, local_sem, y_s, y_r, t_s, f_s, t_r, a_s, b_s, b_r, g_s, r_r, h_s, h_r, c_s, d_s, c_r, q_s, q_r, x_s, x_r,
 ):
     groups, seqs, tokens, feat = dims
     heads = feat // HD
@@ -126,6 +126,12 @@
 
     load_spatial = pltpu.make_async_copy(sp_ref.at[0, 0], spv, local_sem.at[0])
     load_spatial.start()
+    counts = [
+        pltpu.make_async_copy(fc_hbm, fc_ref, scalar_sem.at[0]),
+        pltpu.make_async_copy(cl_hbm, cl_ref, scalar_sem.at[1]),
+    ]
+    for copy in counts:
+        copy.start()
 
     @pl.when(core == 0)
     def _():
@@ -239,6 +245,8 @@
     def own_t(j):
         return pltpu.make_async_copy(tq_ref.at[0, 0, spot_rows(s, j)], trecv.at[j, s], local_sem.at[1 + j])
 
+    for copy in counts:
+        copy.wait()
     frame_total = fc_ref[0]
     caption_total = cl_ref[0]
 
@@ -272,20 +280,21 @@
         def _(dx):
             send(tsend.at[j, x_peer(dx) * 2 + 1 - yl], rrelay.at[j, dx - 1], b_s, b_r.at[j, dx - 1], (g, y_seq))
 
-        send(tsend.at[j, y_seq], tret.at[home], b_s, r_r, (g, y_seq))
-
+        send(tsend.at[j, y_seq], tret.at[home], b_s, r_r.at[j], (g, y_seq))
+
+        tret[home] = tsend[j, s]
+
+    def return_x(j):
         @pl.loop(1, xs)
         def _(dx):
             peer = x_peer(dx) * 2 + yl
-            send(tsend.at[j, peer], tret.at[home], a_s, r_r, (g, peer))
-
-        tret[home] = tsend[j, s]
+            send(tsend.at[j, peer], tret.at[spot_rows(s, j)], a_s, r_r.at[j], (g, peer))
 
     def pass_back(j):
         @pl.loop(1, xs)
         def _(dx):
             landed(rrelay.at[j, dx - 1], b_r.at[j, dx - 1])
-            send(rrelay.at[j, dx - 1], tret.at[spot_rows(y_seq, j)], g_s, r_r, (g, x_peer(dx) * 2 + yl))
+            send(rrelay.at[j, dx - 1], tret.at[spot_rows(y_seq, j)], g_s, r_r.at[j], (g, x_peer(dx) * 2 + yl))
 
     token = lax.broadcasted_iota(jnp.int32, (1, cap_tokens), 1)
     bias = jnp.where(token < caption_total, 0.0, NEG_FILL)
@@ -359,38 +368,54 @@
     pass_z(3)
     spatial(10, 2)
     pass_x(3)
+    return_x(0)
+    return_x(1)
     send_cross(0)
     temporal(2)
+    return_x(2)
     cross_theirs(1)
     send_cross(1)
     pass_back(0)
     temporal(3)
+    return_x(3)
     cross_mine(0)
     pass_back(1)
     cross_mine(1)
-    pass_back(2)
     cross_theirs(2)
     send_cross(2)
+    pass_back(2)
     pass_back(3)
     cross_theirs(3)
     send_cross(3)
     cross_mine(2)
     cross_mine(3)
 
-    landed(tret.at[pl.ds(0, tokens - spots)], r_r)
     keep_frame = (s + jnp.zeros((1, 1), jnp.int32)) < frame_total
 
-    def write(lanes, extra):
-        total = acc[:, lanes] + tret[:, lanes].astype(jnp.float32)
+    def write(rows, lanes, extra):
+        total = acc[rows, lanes] + tret[rows, lanes].astype(jnp.float32)
         if extra is not None:
             total += extra
-        out_ref[0, 0, :, lanes] = jnp.where(keep_frame, total, 0.0).astype(jnp.bfloat16)
-
-    for i in range(SETS):
-        write(pl.ds(col(mine[i]), PAIR), None)
-    for p, (i, first, count) in enumerate(PARCELS):
+        out_ref[0, 0, rows, lanes] = jnp.where(keep_frame, total, 0.0).astype(jnp.bfloat16)
+
+    *early, last = range(len(PARCELS))
+    for p in early:
+        i, first, count = PARCELS[p]
         landed(xret.at[i, :, lanes_of(p)], x_r.at[p])
-        write(pl.ds(col(theirs[i] + first), count * HD), xret[i, :, lanes_of(p)].astype(jnp.float32))
+        acc[:, pl.ds(col(theirs[i] + first), count * HD)] += xret[i, :, lanes_of(p)].astype(jnp.float32)
+    last_set, last_head, _ = PARCELS[last]
+    for j in range(chunks):
+        landed(tret.at[pl.ds(0, (seqs - 1) * ROWS_T)], r_r.at[j])
+
+        @pl.loop(0, seqs)
+        def _(n):
+            rows = spot_rows(n, j)
+            for i in range(SETS):
+                write(rows, pl.ds(col(mine[i]), PAIR), None)
+                write(rows, pl.ds(col(theirs[i]), HD if i == last_set else PAIR), None)
+
+    landed(xret.at[last_set, :, lanes_of(last)], x_r.at[last])
+    write(pl.ds(0, tokens), pl.ds(col(theirs[last_set] + last_head), HD), xret[last_set, :, lanes_of(last)].astype(jnp.float32))
 
     landed(trecv.at[:, pl.ds(0, xs)], y_s)
     landed(trecv.at[:, pl.ds(0, xs - 1)], t_s)
@@ -417,7 +442,7 @@
     return pl.pallas_call(
         functools.partial(kernel, dims),
         out_shape=pltpu.VMEM((1, 1, tokens, feat), bf16),
-        in_specs=[pl.BlockSpec(memory_space=pltpu.SMEM)] * 2 + [pl.BlockSpec(memory_space=pl.ANY)] * 3,
+        in_specs=[pl.BlockSpec(memory_space=pl.ANY)] * 5,
         out_specs=pl.BlockSpec(memory_space=pltpu.VMEM),
         scratch_shapes=[
             pltpu.VMEM((tokens, 3 * feat), bf16),
@@ -432,12 +457,15 @@
             pltpu.VMEM((SETS, tokens, PAIR), bf16),
             pltpu.VMEM((SETS, tokens, PAIR), bf16),
             pltpu.VMEM((tokens, feat), jnp.float32),
+            pltpu.SMEM((1,), jnp.int32),
+            pltpu.SMEM((1,), jnp.int32),
             pltpu.SemaphoreType.REGULAR,
             pltpu.SemaphoreType.REGULAR,
+            dma((2,)),
             dma((1 + chunks + 2 * SETS + len(PARCELS),)),
             dma, dma((chunks, seqs // 2 - 1)),
             dma, dma, dma((chunks,)),
-            dma, dma, dma((chunks, seqs // 2 - 1)), dma, dma,
+            dma, dma, dma((chunks, seqs // 2 - 1)), dma, dma((chunks,)),
             dma, dma((len(PARCELS),)),
             dma, dma, dma((len(PARCELS),)),
             dma, dma((SETS,)),

time: 91.5 us -> 91.3 us (level)
  no operation moved by 1% of the time
where the time goes in v5:
time: 91.3 us; the launch traced here: 91.2 us
  Pallas kernels  88.8 us (97%)
  between operations  1.31 us (1%)
  local copies, waits for them, and re-layouts  1.15 us (1%)
    pallas_call x1, Pallas kernels, body(): pl.pallas_call(functools.partial(kernel, dims), out_shape=pltpu.VMEM((1,...  88.8 us

profile of v5, /device:TPU:1, one launch (start us, length us, event | category | flops | bytes accessed | tf_op | source)
XLA Modules:
  0.0 91.2 jit_solution(16338638219571237936)
XLA Ops:
  1.3 88.8 %shard_map.55 = bf16[1,1,512,1536]{3,2,1,0:T(8,128)(2,1)S(1)} custom-call(s32[1]{0:T(128)S(6)} %copy.8.fc_hbm, s32[1]{0:T(128)S(6)} %copy.9.cl_hbm, bf16[1,1,512,4608]{3,2,1,0:T(8,128)(2,1)} %sp_ref.1, bf16[1,1,512,4608]{3,2,1,0:T(8,128)(2,1)} %tq_ref.1, bf16[8,2,2,32,3072]{4,3,2,1,0:T(8,128)(2,1)} %bitcast.1), custom_call_target="tpu_custom_call" | custom-call | tf_op jit(solution)/shard_map/pallas_call | solution.py:442
  90.1 1.1 %copy.7 = bf16[1,1,512,1536]{3,2,1,0:T(8,128)(2,1)} copy(bf16[1,1,512,1536]{3,2,1,0:T(8,128)(2,1)S(1)} %shard_map.55) | data formatting | bytes 3145728
